TPU v7x, 256 devices: a whole 4x4x8 slice. The times are simulated.
256 devices in a mesh: ctx: 128 (over x_hi, z, y, core), tp: 2 (over x_lo).
Axes of the slice: x: 4 (x_hi: 2, x_lo: 2; x = x_hi * 2 + x_lo), y: 4, z: 8, core: 2. Of those that a mesh axis runs over, the one named last changes fastest.
Arguments:
- query: bfloat16 [32768, 2048], P('ctx', 'tp'), may hold values from -6 to 6
- key_in: bfloat16 [32768, 2048], P('ctx', 'tp'), may hold values from -6 to 6
- value: bfloat16 [32768, 2048], P('ctx', 'tp'), may hold values from -6 to 6
- grad_out: bfloat16 [32768, 2048], P('ctx', 'tp'), may hold values from -6 to 6
- residue: float32 [16, 2048], P(None, 'tp'), may hold values from -0.125 to 0.125
- rate: float32 [16, 2048], P(None, 'tp'), may hold values from 0.5 to 1024
Outputs:
- grad_query: bfloat16 [32768, 2048], P('ctx', 'tp')
- grad_key: bfloat16 [32768, 2048], P('ctx', 'tp')
- grad_value: bfloat16 [32768, 2048], P('ctx', 'tp')
- grad_residue: float32 [16, 2048], P(None, 'tp')
- grad_rate: float32 [16, 2048], P(None, 'tp')
All inputs are finite; a program needn't handle non-finite values.
Results may differ from a plain program's by a relative error of at most 0.0058.
Values may be sent and summed in bfloat16 or wider, within the bound.
A program may use at most 320 MiB of HBM per device.

v0:
```python
from functools import partial
import jax
import jax.numpy as jnp
from jax import lax
from jax.sharding import PartitionSpec as P

BLK = 128
HIGH = lax.Precision.HIGHEST


def combine_fwd(lam, earlier, later):
    span_a, state_a, moment_a = earlier
    span_b, state_b, moment_b = later
    decay = jnp.exp(-lam * span_b)
    return (
        span_a + span_b,
        decay * state_a + state_b,
        decay * (moment_a + span_b * state_a) + moment_b,
    )


def combine_rev(lam, earlier, later):
    span_a, state_a = earlier
    span_b, state_b = later
    return (span_a + span_b, jnp.exp(-lam * span_b) * state_a + state_b)


def layouts():
    return ("cbj", "cbi", "cmb", 2)


def prepare(gated, grad_conv, rate, seq_len):
    lay_j, lay_i, lay_s, axis_b = layouts()
    lam = rate / seq_len
    pos = jnp.arange(BLK, dtype=jnp.float32)[:, None, None]
    head = jnp.exp(-lam * pos)
    head_next = jnp.exp(-lam * (pos + 1.0))
    tail = jnp.exp(-lam * (BLK - 1.0 - pos))
    back = jnp.exp(-lam * (BLK - pos))
    chans, rows = gated.shape
    blocks = rows // BLK
    gated_b = gated.astype(jnp.float32).reshape(chans, blocks, BLK)
    grad_b = grad_conv.astype(jnp.float32).reshape(chans, blocks, BLK)
    lam_s = lam.T[:, :, None]
    spans = jnp.full((1, 1, blocks), float(BLK), jnp.float32)
    state_sum = jnp.einsum(lay_j + ",jmc->" + lay_s, gated_b, tail, precision=HIGH)
    moment_sum = jnp.einsum(
        lay_j + ",jmc->" + lay_s, gated_b, (BLK - 1.0 - pos) * tail, precision=HIGH
    )
    back_sum = jnp.einsum(lay_i + ",imc->" + lay_s, grad_b, head, precision=HIGH)
    fwd_incl = lax.associative_scan(
        partial(combine_fwd, lam_s), (spans, state_sum, moment_sum), axis=axis_b
    )
    rev_incl = lax.associative_scan(
        partial(combine_rev, lam_s), (spans, back_sum), reverse=True, axis=axis_b
    )
    tables = (lam_s, pos, head, head_next, back)
    return (tables, gated_b, grad_b, fwd_incl, rev_incl)


def shift_down(arr, axis_b):
    count = arr.shape[axis_b]
    first = jnp.zeros_like(lax.slice_in_dim(arr, 0, 1, axis=axis_b))
    return jnp.concatenate([first, lax.slice_in_dim(arr, 0, count - 1, axis=axis_b)], axis_b)


def shift_up(arr, axis_b):
    count = arr.shape[axis_b]
    last = jnp.zeros_like(lax.slice_in_dim(arr, 0, 1, axis=axis_b))
    return jnp.concatenate([lax.slice_in_dim(arr, 1, count, axis=axis_b), last], axis_b)


def finish(tables, gated_b, grad_b, fwd_incl, rev_incl, fwd_in, rev_in, residue, seq_len):
    lam_s, pos, head, head_next, back = tables
    lay_j, lay_i, lay_s, axis_b = layouts()
    fwd_excl = tuple((shift_down(part, axis_b) for part in fwd_incl))
    rev_excl = tuple((shift_up(part, axis_b) for part in rev_incl))
    _, state_in, moment_in = combine_fwd(lam_s, fwd_in, fwd_excl)
    _, back_in = combine_rev(lam_s, rev_in, rev_excl)
    lag = jnp.arange(BLK)
    onehot = (lag[:, None, None] - lag[None, :, None] == lag[None, None, :]).astype(jnp.float32)
    short_filter = jnp.einsum("mc,kmc->kc", residue, head, precision=HIGH)
    toeplitz = jnp.einsum("kc,ijk->cij", short_filter, onehot, precision=HIGH)
    conv = jnp.einsum("cij," + lay_j + "->" + lay_i, toeplitz, gated_b, precision=HIGH)
    conv = conv + jnp.einsum(
        "imc," + lay_s + "->" + lay_i, residue * head_next, state_in, precision=HIGH
    )
    grad_gated = jnp.einsum("cij," + lay_i + "->" + lay_j, toeplitz, grad_b, precision=HIGH)
    grad_gated = grad_gated + jnp.einsum(
        "jmc," + lay_s + "->" + lay_j, residue * back, back_in, precision=HIGH
    )
    outer = jnp.einsum(lay_i + "," + lay_j + "->cij", grad_b, gated_b, precision=HIGH)
    correl = jnp.einsum("cij,ijk->kc", outer, onehot, precision=HIGH)
    near_w = jnp.einsum(lay_i + ",imc->" + lay_s, grad_b, head_next, precision=HIGH)
    near_t = jnp.einsum(lay_i + ",imc->" + lay_s, grad_b, (pos + 1.0) * head_next, precision=HIGH)
    pair = lay_s + "," + lay_s + "->mc"
    grad_residue = jnp.einsum("kc,kmc->mc", correl, head, precision=HIGH)
    grad_residue = grad_residue + jnp.einsum(pair, near_w, state_in, precision=HIGH)
    weighted = jnp.einsum("kc,kmc->mc", correl, pos * head, precision=HIGH)
    weighted = weighted + jnp.einsum(pair, near_t, state_in, precision=HIGH)
    weighted = weighted + jnp.einsum(pair, near_w, moment_in, precision=HIGH)
    grad_rate = -residue / seq_len * weighted
    scale = seq_len ** (-0.5)
    chans = conv.shape[0]
    rows = conv.shape[1] * BLK
    shape_out = (chans, rows)
    return (
        conv.reshape(shape_out).astype(jnp.bfloat16),
        grad_gated.reshape(shape_out).astype(jnp.bfloat16),
        scale * grad_residue,
        scale * grad_rate,
    )


def local(query, key_in, value, grad_out, residue, rate):
    gated = (key_in.astype(jnp.float32) * value.astype(jnp.float32)).astype(jnp.bfloat16)
    grad_conv = (grad_out.astype(jnp.float32) * query.astype(jnp.float32)).astype(jnp.bfloat16)
    gated_t = gated.T
    grad_t = grad_conv.T
    gated_ch, grad_ch = (
        lax.all_to_all(gated_t, "ctx", split_axis=0, concat_axis=1, tiled=True),
        lax.all_to_all(grad_t, "ctx", split_axis=0, concat_axis=1, tiled=True),
    )
    chans = gated_ch.shape[0]
    seq_len = gated_ch.shape[1]
    start = lax.axis_index("ctx") * chans
    residue_ch = lax.dynamic_slice_in_dim(residue, start, chans, 1)
    rate_ch = lax.dynamic_slice_in_dim(rate, start, chans, 1)
    tables, gated_b, grad_b, fwd_incl, rev_incl = prepare(gated_ch, grad_ch, rate_ch, seq_len)
    zero_span = jnp.zeros((1, 1, 1), jnp.float32)
    zero_state = jnp.zeros((1, 1, 1), jnp.float32)
    conv_ch, grad_gated_ch, own_res, own_rate = finish(
        tables,
        gated_b,
        grad_b,
        fwd_incl,
        rev_incl,
        (zero_span, zero_state, zero_state),
        (zero_span, zero_state),
        residue_ch,
        seq_len,
    )
    conv_t, grad_gated_t = (
        lax.all_to_all(conv_ch, "ctx", split_axis=1, concat_axis=0, tiled=True),
        lax.all_to_all(grad_gated_ch, "ctx", split_axis=1, concat_axis=0, tiled=True),
    )
    conv = conv_t.T
    grad_gated = grad_gated_t.T
    grad_residue, grad_rate = (
        lax.all_gather(own_res, "ctx", axis=1, tiled=True),
        lax.all_gather(own_rate, "ctx", axis=1, tiled=True),
    )
    conv_f = conv.astype(jnp.float32)
    grad_gated_f = grad_gated.astype(jnp.float32)
    grad_query = (grad_out.astype(jnp.float32) * conv_f).astype(jnp.bfloat16)
    grad_key = (grad_gated_f * value.astype(jnp.float32)).astype(jnp.bfloat16)
    grad_value = (grad_gated_f * key_in.astype(jnp.float32)).astype(jnp.bfloat16)
    return (grad_query, grad_key, grad_value, grad_residue, grad_rate)


def solution(mesh):
    in_specs = (
        P("ctx", "tp"),
        P("ctx", "tp"),
        P("ctx", "tp"),
        P("ctx", "tp"),
        P(None, "tp"),
        P(None, "tp"),
    )
    out_specs = (P("ctx", "tp"), P("ctx", "tp"), P("ctx", "tp"), P(None, "tp"), P(None, "tp"))
    return jax.shard_map(local, mesh=mesh, in_specs=in_specs, out_specs=out_specs, check_vma=False)
```

profile of v0, /device:TPU:1, one launch (start us, length us, event | category | flops | bytes accessed | tf_op | source)
XLA Modules:
  0.0 864.4 jit_solution(11036327460467527053)
XLA Ops:
  3.1 17.0 %all-to-all-start.2 = ((bf16[128,8,256]{2,1,0:T(8,128)(2,1)}), bf16[128,8,256]{2,1,0:T(8,128)(2,1)S(1)}, u32[]{:S(2)}, u32[]{:S(2)}) async-start(bf16[128,8,256]{2,1,0:T(8,128)(2,1)} %fusion.14), calls=%async_computation.2 | async-start | bytes 1048576 | tf_op jit(solution)/shard_map/all_to_all | solution.py:122
  21.5 6.5 fusion.1
  28.0 14.1 %all-to-all-done.2 = bf16[128,8,256]{2,1,0:T(8,128)(2,1)S(1)} async-done(((bf16[128,8,256]{2,1,0:T(8,128)(2,1)}), bf16[128,8,256]{2,1,0:T(8,128)(2,1)S(1)}, u32[]{:S(2)}, u32[]{:S(2)}) %all-to-all-start.2) | async-done | bytes 524320 | tf_op jit(solution)/shard_map/all_to_all | solution.py:122
  42.9 2.2 slice.423
  45.1 2.2 slice.425
  49.5 2.2 slice.460
  53.7 44.0 %pad.368 = f32[8,16,256]{1,0,2:T(8,128)S(1)} pad(f32[8,16,128]{1,0,2:T(8,128)} %add.470, f32[]{:T(128)} %constant.112.clone.1), padding=0_0_0x0_0_0x1_0_1 | pad | bytes 196612
  98.7 1.9 fusion.18
  100.7 1.9 pad_maximum_fusion.1
  102.6 44.0 %pad.279 = f32[8,16,255]{1,0,2:T(8,128)S(1)} pad(f32[8,16,128]{1,0,2:T(8,128)} %pad_maximum_fusion.1, f32[]{:T(128)} %constant.112.clone.1), padding=0_0_0x0_0_0x0_0_1 | pad | bytes 196100 | tf_op jit(solution)/shard_map/slice | solution.py:70
  147.7 1.3 slice.463
  152.5 5.8 all-to-all-start.3
  159.5 20.9 %all-to-all-done.3 = bf16[8,128,256]{2,0,1:T(8,128)(2,1)S(1)} async-done(((bf16[8,128,256]{2,0,1:T(8,128)(2,1)}), bf16[8,128,256]{2,0,1:T(8,128)(2,1)S(1)}, u32[]{:S(2)}, u32[]{:S(2)}) %all-to-all-start.3) | async-done | bytes 524320 | tf_op jit(solution)/shard_map/all_to_all | solution.py:145
  180.5 2.1 fusion.8
  182.6 5.5 all-to-all-start
  188.7 1.3 copy.239
  193.9 16.3 %all-to-all-done = bf16[128,8,256]{2,1,0:T(8,128)(2,1)S(1)} async-done(((bf16[128,8,256]{2,1,0:T(8,128)(2,1)}), bf16[128,8,256]{2,1,0:T(8,128)(2,1)S(1)}, u32[]{:S(2)}, u32[]{:S(2)}) %all-to-all-start) | async-done | bytes 524320 | tf_op jit(solution)/shard_map/all_to_all | solution.py:121
  211.1 2.2 slice.385
  213.3 2.2 slice.386
  216.1 2.2 slice.465
  218.3 2.2 slice.466
  223.8 1.5 multiply_add_fusion
  230.4 1.9 pad.186
  232.3 1.9 pad.187
  234.1 1.9 pad.219
  237.3 1.9 pad.218
  239.2 1.3 add.434
  240.5 1.4 fusion.68
  245.2 3.1 pad.188
  248.4 3.1 pad.189
  252.8 3.1 pad.220
  256.0 3.1 pad.221
  259.1 1.4 add.436
  260.5 1.4 fusion.65
  261.9 1.4 add.499
  266.4 4.6 pad.190
  270.9 4.5 pad.191
  275.5 4.6 pad.223
  280.0 1.4 pad_maximum_fusion.14
  281.4 4.5 pad.222
  285.9 1.5 add.438
  287.4 1.6 fusion.44
  289.0 1.5 add.502
  291.9 5.5 pad.193
  297.3 1.5 pad_maximum_fusion.11
  298.8 8.3 pad.224
  307.1 8.3 pad.225
  316.1 1.7 fusion.27
  320.1 10.9 %pad.227 = f32[8,16,64]{1,0,2:T(8,128)S(1)} pad(f32[8,16,32]{1,0,2:T(8,128)} %add.505, f32[]{:T(128)} %constant.112.clone.1), padding=0_0_0x0_0_0x1_0_1 | pad | bytes 49156 | tf_op jit(solution)/shard_map/pad | solution.py:51
  331.0 1.5 pad_maximum_fusion.8
  332.5 15.0 %pad.226 = f32[8,16,64]{1,0,2:T(8,128)} pad(f32[8,16,32]{1,0,2:T(8,128)} %pad_maximum_fusion.8, f32[]{:T(128)} %constant.112.clone.1), padding=0_0_0x0_0_0x0_1_1 | pad | bytes 49156 | tf_op jit(solution)/shard_map/pad | solution.py:51
  347.5 1.7 add.508
  349.2 1.8 fusion.24
  351.7 2.2 slice.420
  353.9 3.1 slice.500
  358.2 1.6 fusion.21
  361.3 38.7 %pad.369 = f32[8,16,256]{1,0,2:T(8,128)} pad(f32[8,16,128]{1,0,2:T(8,128)S(1)} %add.511, f32[]{:T(128)} %constant.112.clone.1), padding=0_0_0x0_0_0x1_0_1 | pad | bytes 196612
  405.1 38.7 %pad.281 = f32[8,16,255]{1,0,2:T(8,128)} pad(f32[8,16,128]{1,0,2:T(8,128)S(1)} %pad_maximum_fusion.2, f32[]{:T(128)} %constant.112.clone.1), padding=0_0_0x0_0_0x0_0_1 | pad | bytes 196100 | tf_op jit(solution)/shard_map/slice | solution.py:64
  445.0 38.7 %pad.277 = f32[8,16,255]{1,0,2:T(8,128)} pad(f32[8,16,128]{1,0,2:T(8,128)S(1)} %pad_maximum_fusion, f32[]{:T(128)} %constant.112.clone.1), padding=0_0_0x0_0_0x0_0_1 | pad | bytes 196100 | tf_op jit(solution)/shard_map/slice | solution.py:64
  483.7 3.4 fusion
  491.5 5.7 all-to-all-start.1
  497.2 1.5 slice_add_fusion.33
  499.8 184.7 %all_gather.7 = f32[16,1024]{0,1:T(8,128)S(1)} all-gather(f32[16,8]{0,1:T(8,128)S(1)} %multiply_multiply_fusion), channel_id=1, replica_groups=mesh['ctx'=128,'tp'=2] {'ctx'}, dimensions={1}, use_global_device_ids=true | all-gather | bytes 66048 | tf_op jit(solution)/shard_map/all_gather | solution.py:151
  685.6 176.6 %all_gather.6 = f32[16,1024]{0,1:T(8,128)S(1)} all-gather(f32[16,8]{0,1:T(8,128)S(1)} %add_multiply_fusion.6), channel_id=1, replica_groups=mesh['ctx'=128,'tp'=2] {'ctx'}, dimensions={1}, use_global_device_ids=true | all-gather | bytes 66048 | tf_op jit(solution)/shard_map/all_gather | solution.py:150
  (260 shorter events, 60.5 us)
Async XLA Ops:
  0.6 1.3 copy-start.21
  3.1 39.0 %all-to-all-start.2 = ((bf16[128,8,256]{2,1,0:T(8,128)(2,1)}), bf16[128,8,256]{2,1,0:T(8,128)(2,1)S(1)}, u32[]{:S(2)}, u32[]{:S(2)}) async-start(bf16[128,8,256]{2,1,0:T(8,128)(2,1)} %fusion.14), calls=%async_computation.2 | async-start | bytes 1048576 | tf_op jit(solution)/shard_map/all_to_all | solution.py:122
  21.1 129.0 %copy-start.39 = (f32[16,8]{0,1:T(8,128)}, f32[16,8]{0,1:T(8,128)S(1)}, u32[]{:S(2)}) copy-start(f32[16,8]{0,1:T(8,128)S(1)} %copy.254) | copy-start | bytes 1540
  21.1 6.9 copy-start.41
  21.1 128.5 %copy-start.37 = (f32[8,16]{1,0:T(8,128)}, f32[8,16]{1,0:T(8,128)S(1)}, u32[]{:S(2)}) copy-start(f32[8,16]{1,0:T(8,128)S(1)} %get-tuple-element.84) | copy-start | bytes 1540
  21.4 26.6 %copy-start.43 = (f32[8,16]{1,0:T(8,128)}, f32[8,16]{1,0:T(8,128)S(1)}, u32[]{:S(2)}) copy-start(f32[8,16]{1,0:T(8,128)S(1)} %get-tuple-element.86) | copy-start | bytes 1540
  21.4 26.8 %copy-start.35 = (f32[8,16]{1,0:T(8,128)}, f32[8,16]{1,0:T(8,128)S(1)}, u32[]{:S(2)}) copy-start(f32[8,16]{1,0:T(8,128)S(1)} %get-tuple-element.87) | copy-start | bytes 1540
  21.4 26.9 %copy-start.33 = (f32[8,16]{1,0:T(8,128)}, f32[8,16]{1,0:T(8,128)S(1)}, u32[]{:S(2)}) copy-start(f32[8,16]{1,0:T(8,128)S(1)} %get-tuple-element.88) | copy-start | bytes 1540
  21.4 27.1 %copy-start.31 = (f32[8,16]{1,0:T(8,128)}, f32[8,16]{1,0:T(8,128)S(1)}, u32[]{:S(2)}) copy-start(f32[8,16]{1,0:T(8,128)S(1)} %get-tuple-element.89) | copy-start | bytes 1540
  21.5 27.4 %copy-start.28 = (f32[8,16]{1,0:T(8,128)}, f32[8,16]{1,0:T(8,128)S(1)}, u32[]{:S(2)}) copy-start(f32[8,16]{1,0:T(8,128)S(1)} %get-tuple-element.90) | copy-start | bytes 1540
  47.9 1.5 copy-start.5
  49.5 2.3 slice-start
  147.7 1.4 copy-start.7
  149.0 0.7 copy-start.50
  151.4 6.9 copy-start.22
  152.5 6.0 copy-start.23
  152.5 27.9 %all-to-all-start.3 = ((bf16[8,128,256]{2,0,1:T(8,128)(2,1)}), bf16[8,128,256]{2,0,1:T(8,128)(2,1)S(1)}, u32[]{:S(2)}, u32[]{:S(2)}) async-start(bf16[8,128,256]{2,0,1:T(8,128)(2,1)} %copy.217), calls=%async_computation.3 | async-start | bytes 1048576 | tf_op jit(solution)/shard_map/all_to_all | solution.py:145
  182.6 27.6 %all-to-all-start = ((bf16[128,8,256]{2,1,0:T(8,128)(2,1)}), bf16[128,8,256]{2,1,0:T(8,128)(2,1)S(1)}, u32[]{:S(2)}, u32[]{:S(2)}) async-start(bf16[128,8,256]{2,1,0:T(8,128)(2,1)} %get-tuple-element.53), calls=%async_computation | async-start | bytes 1048576 | tf_op jit(solution)/shard_map/all_to_all | solution.py:121
  188.1 2.5 copy-start.47
  211.1 146.0 %copy-start.11 = (f32[8,16,256]{2,1,0:T(8,128)}, f32[8,16,256]{2,1,0:T(8,128)S(1)}, u32[]{:S(2)}) copy-start(f32[8,16,256]{2,1,0:T(8,128)S(1)} %fusion.39) | copy-start | bytes 393220
  216.1 6.7 copy-start.12
  225.3 0.7 copy-start.29
  225.3 0.7 copy-start.32
  225.3 1.4 copy-start.34
  225.4 1.3 copy-start.36
  225.4 1.4 copy-start.44
  226.0 0.6 copy-start.24
  226.0 0.6 copy-start.25
  226.7 2.5 copy-start.26
  226.7 3.1 copy-start.27
  287.4 28.6 %copy-start.30 = (f32[8,16]{1,0:T(8,128)S(1)}, f32[8,16]{1,0:T(8,128)}, u32[]{:S(2)}) copy-start(f32[8,16]{1,0:T(8,128)} %copy-done.28) | copy-start | bytes 1540
  315.4 2.3 copy-start.13
  315.4 2.3 copy-start.14
  315.4 4.2 copy-start.46
  317.7 2.1 copy-start.20
  351.7 6.5 copy-start.8
  358.2 1.6 copy-start.18
  358.2 1.6 copy-start.45
  359.8 0.9 copy-start.16
  361.3 38.7 %copy-start.17 = (f32[8,16,63]{1,0,2:T(8,128)S(1)}, f32[8,16,63]{1,0,2:T(8,128)}, u32[]{:S(2)}) copy-start(f32[8,16,63]{1,0,2:T(8,128)} %get-tuple-element.46) | copy-start | bytes 96772
  400.0 1.0 copy-start.15
  400.9 1.8 slice-start.2
  402.9 1.2 copy-start.10
  405.1 38.8 %copy-start.6 = (f32[8,16,128]{1,0,2:T(8,128)S(1)}, f32[8,16,128]{1,0,2:T(8,128)}, u32[]{:S(2)}) copy-start(f32[8,16,128]{1,0,2:T(8,128)} %add.444) | copy-start | bytes 196612
  443.8 1.0 slice-start.1
  443.8 1.1 copy-start.9
  444.9 38.8 %copy-start.19 = (f32[8,128,128]{2,1,0:T(8,128)S(1)}, f32[8,128,128]{2,1,0:T(8,128)}, u32[]{:S(2)}) copy-start(f32[8,128,128]{2,1,0:T(8,128)} %fusion.83) | copy-start | bytes 1572868
  444.9 38.8 %copy-start.42 = (s32[128,128]{1,0:T(8,128)S(1)}, s32[128,128]{1,0:T(8,128)}, u32[]{:S(2)}) copy-start(s32[128,128]{1,0:T(8,128)} %copy-done.41) | copy-start | bytes 196612
  483.7 3.4 copy-start.4
  487.1 0.7 copy-start.38
  487.1 0.7 copy-start.49
  487.8 1.2 copy-start.2
  487.8 1.2 copy-start.40
  487.8 1.2 copy-start.48
  490.4 6.8 copy-start.3
  491.5 371.5 %all-to-all-start.1 = ((bf16[8,128,256]{2,0,1:T(8,128)(2,1)}), bf16[8,128,256]{2,0,1:T(8,128)(2,1)S(1)}, u32[]{:S(2)}, u32[]{:S(2)}) async-start(bf16[8,128,256]{2,0,1:T(8,128)(2,1)} %copy.208), calls=%async_computation.1 | async-start | bytes 1048576 | tf_op jit(solution)/shard_map/all_to_all | solution.py:144
  497.2 1.8 copy-start
  497.2 1.8 copy-start.1
where the time goes:
time: 876 us; the launch traced here: 864 us
  blocking collectives  361 us (41%)
  local copies, waits for them, and re-layouts  348 us (40%)
  waiting for transfers between devices  51.4 us (6%)
  other arithmetic  48.1 us (5%)
  starting transfers between devices  34 us (4%)
  matrix products  19.2 us (2%)
    all_gather x1, blocking collectives, local(): lax.all_gather(own_rate, 'ctx', axis=1, tiled=True)  185 us
    all_gather x1, blocking collectives, local(): lax.all_gather(own_res, 'ctx', axis=1, tiled=True)  177 us
    unnamed x130, local copies, waits for them, and re-layouts  104 us
    pad x24, local copies, waits for them, and re-layouts, prepare(): lax.associative_scan(partial(combine_fwd, lam_s), (spans, state_sum, mome...  88.6 us
    slice x2, local copies, waits for them, and re-layouts, shift_down(): lax.slice_in_dim(arr, 0, count - 1, axis=axis_b)  77.4 us
    slice x2, local copies, waits for them, and re-layouts, shift_up(): lax.slice_in_dim(arr, 1, count, axis=axis_b)  45.3 us
    all_to_all x1, waiting for transfers between devices, local(): lax.all_to_all(grad_gated_ch, 'ctx', split_axis=1, concat_axis=0, tiled=T...  20.9 us
    slice x20, local copies, waits for them, and re-layouts, prepare(): lax.associative_scan(partial(combine_fwd, lam_s), (spans, state_sum, mome...  20.2 us
  transfers between devices with their start and end apart: 4, of which 3 were waited for; matrix products, arithmetic and copies ran while one was open for 2% of the time, Pallas kernels for 0%

commit v1 on v0

--- a/solution.py
+++ b/solution.py
@@ -147,7 +147,9 @@
     conv = conv_t.T
     grad_gated = grad_gated_t.T
     grad_residue, grad_rate = (
-        lax.all_gather(own_res, "ctx", axis=1, tiled=True),
+        jnp.concatenate(
+            lax.all_to_all(jnp.stack([own_res] * lax.axis_size("ctx")), "ctx", 0, 0), axis=1
+        ),
         lax.all_gather(own_rate, "ctx", axis=1, tiled=True),
     )
     conv_f = conv.astype(jnp.float32)

time: 876 us -> 684 us (0.78)
  blocking collectives: 361 us -> 185 us
  local copies, waits for them, and re-layouts: 348 us -> 314 us
  waiting for transfers between devices: 51.4 us -> 64 us
    all_gather x1 -> x0, blocking collectives: 177 us -> none  [local(): lax.all_gather(own_res, 'ctx', axis=1, tiled=True)]
    slice x2, local copies, waits for them, and re-layouts: 77.4 us -> 39.7 us  [shift_down(): lax.slice_in_dim(arr, 0, count - 1, axis=axis_b)]
    all_to_all x0 -> x1, waiting for transfers between devices: none -> 9.87 us  [local(): lax.all_to_all(jnp.stack([own_res] * lax.axis_size('ctx')), 'ctx', 0, 0)]
    unnamed x130 -> x131, local copies, waits for them, and re-layouts: 104 us -> 107 us
  transfers between devices with their start and end apart: 4 -> 5, of which waited for: 3 -> 4; matrix products, arithmetic and copies ran while one was open for 2% -> 3% of each run, Pallas kernels for 0% -> 0%
where the time goes in v1:
time: 684 us; the launch traced here: 672 us
  local copies, waits for them, and re-layouts  314 us (46%)
  blocking collectives  185 us (27%)
  waiting for transfers between devices  64 us (9%)
  other arithmetic  46.5 us (7%)
  starting transfers between devices  39.8 us (6%)
  matrix products  20.4 us (3%)
    all_gather x1, blocking collectives, local(): lax.all_gather(own_rate, 'ctx', axis=1, tiled=True)  185 us
    unnamed x131, local copies, waits for them, and re-layouts  107 us
    pad x24, local copies, waits for them, and re-layouts, prepare(): lax.associative_scan(partial(combine_fwd, lam_s), (spans, state_sum, mome...  88.5 us
    slice x2, local copies, waits for them, and re-layouts, shift_up(): lax.slice_in_dim(arr, 1, count, axis=axis_b)  45.3 us
    slice x2, local copies, waits for them, and re-layouts, shift_down(): lax.slice_in_dim(arr, 0, count - 1, axis=axis_b)  39.7 us
    all_to_all x1, waiting for transfers between devices, local(): lax.all_to_all(grad_gated_ch, 'ctx', split_axis=1, concat_axis=0, tiled=T...  21.7 us
    slice x20, local copies, waits for them, and re-layouts, prepare(): lax.associative_scan(partial(combine_fwd, lam_s), (spans, state_sum, mome...  20.3 us
    all_to_all x1, waiting for transfers between devices, local(): lax.all_to_all(gated_t, 'ctx', split_axis=0, concat_axis=1, tiled=True)  18.3 us
  transfers between devices with their start and end apart: 5, of which 4 were waited for; matrix products, arithmetic and copies ran while one was open for 3% of the time, Pallas kernels for 0%

profile of v1, /device:TPU:1, one launch (start us, length us, event | category | flops | bytes accessed | tf_op | source)
XLA Modules:
  0.0 671.7 jit_solution(9820914066035875867)
XLA Ops:
  3.1 17.0 %all-to-all-start.2 = ((bf16[128,8,256]{2,1,0:T(8,128)(2,1)}), bf16[128,8,256]{2,1,0:T(8,128)(2,1)S(1)}, u32[]{:S(2)}, u32[]{:S(2)}) async-start(bf16[128,8,256]{2,1,0:T(8,128)(2,1)} %fusion.14), calls=%async_computation.2 | async-start | bytes 1048576 | tf_op jit(solution)/shard_map/all_to_all | solution.py:122
  21.5 6.5 fusion.1
  28.0 14.1 %all-to-all-done.2 = bf16[128,8,256]{2,1,0:T(8,128)(2,1)S(1)} async-done(((bf16[128,8,256]{2,1,0:T(8,128)(2,1)}), bf16[128,8,256]{2,1,0:T(8,128)(2,1)S(1)}, u32[]{:S(2)}, u32[]{:S(2)}) %all-to-all-start.2) | async-done | bytes 524320 | tf_op jit(solution)/shard_map/all_to_all | solution.py:122
  42.9 2.2 slice.423
  45.1 2.2 slice.425
  49.5 2.2 slice.460
  53.7 44.0 %pad.368 = f32[8,16,256]{1,0,2:T(8,128)S(1)} pad(f32[8,16,128]{1,0,2:T(8,128)} %add.470, f32[]{:T(128)} %constant.112.clone.1), padding=0_0_0x0_0_0x1_0_1 | pad | bytes 196612
  98.7 1.9 fusion.18
  100.7 1.9 pad_maximum_fusion.1
  102.6 44.0 %pad.279 = f32[8,16,255]{1,0,2:T(8,128)S(1)} pad(f32[8,16,128]{1,0,2:T(8,128)} %pad_maximum_fusion.1, f32[]{:T(128)} %constant.112.clone.1), padding=0_0_0x0_0_0x0_0_1 | pad | bytes 196100 | tf_op jit(solution)/shard_map/slice | solution.py:70
  147.7 1.3 slice.463
  152.5 5.8 all-to-all-start.3
  158.7 21.7 %all-to-all-done.3 = bf16[8,128,256]{2,0,1:T(8,128)(2,1)S(1)} async-done(((bf16[8,128,256]{2,0,1:T(8,128)(2,1)}), bf16[8,128,256]{2,0,1:T(8,128)(2,1)S(1)}, u32[]{:S(2)}, u32[]{:S(2)}) %all-to-all-start.3) | async-done | bytes 524320 | tf_op jit(solution)/shard_map/all_to_all | solution.py:145
  180.5 1.7 fusion.8
  182.1 5.4 all-to-all-start
  188.2 1.4 copy.239
  191.4 18.3 %all-to-all-done = bf16[128,8,256]{2,1,0:T(8,128)(2,1)S(1)} async-done(((bf16[128,8,256]{2,1,0:T(8,128)(2,1)}), bf16[128,8,256]{2,1,0:T(8,128)(2,1)S(1)}, u32[]{:S(2)}, u32[]{:S(2)}) %all-to-all-start) | async-done | bytes 524320 | tf_op jit(solution)/shard_map/all_to_all | solution.py:121
  210.6 2.2 slice.385
  212.8 2.2 slice.386
  215.6 2.2 slice.465
  217.8 2.2 slice.466
  223.3 1.5 multiply_add_fusion
  229.9 1.9 pad.186
  231.8 1.9 pad.187
  233.6 1.9 pad.219
  236.8 1.9 pad.218
  238.7 1.3 add.434
  240.0 1.4 fusion.68
  241.4 1.3 add.496
  244.7 3.1 pad.188
  247.8 3.1 pad.189
  252.3 3.1 pad.220
  255.4 3.1 pad.221
  258.5 1.4 add.436
  259.9 1.4 fusion.65
  261.4 1.4 add.499
  265.8 4.6 pad.190
  270.4 4.5 pad.191
  274.9 4.5 pad.223
  279.5 1.4 pad_maximum_fusion.14
  280.8 4.5 pad.222
  285.4 1.5 add.438
  286.9 1.6 fusion.44
  288.5 1.5 add.502
  291.4 5.4 pad.193
  296.8 1.5 pad_maximum_fusion.11
  298.3 8.3 %pad.224 = f32[8,16,32]{1,0,2:T(8,128)} pad(f32[8,16,16]{1,0,2:T(8,128)} %pad_maximum_fusion.11, f32[]{:T(128)} %constant.112.clone.1), padding=0_0_0x0_0_0x0_1_1 | pad | bytes 24580 | tf_op jit(solution)/shard_map/pad | solution.py:51
  306.6 8.3 %pad.225 = f32[8,16,32]{1,0,2:T(8,128)} pad(f32[8,16,16]{1,0,2:T(8,128)} %add.502, f32[]{:T(128)} %constant.112.clone.1), padding=0_0_0x0_0_0x1_0_1 | pad | bytes 24580 | tf_op jit(solution)/shard_map/pad | solution.py:51
  315.5 1.7 fusion.27
  319.6 10.9 %pad.227 = f32[8,16,64]{1,0,2:T(8,128)S(1)} pad(f32[8,16,32]{1,0,2:T(8,128)} %add.505, f32[]{:T(128)} %constant.112.clone.1), padding=0_0_0x0_0_0x1_0_1 | pad | bytes 49156 | tf_op jit(solution)/shard_map/pad | solution.py:51
  330.5 1.6 pad_maximum_fusion.8
  332.0 14.9 %pad.226 = f32[8,16,64]{1,0,2:T(8,128)} pad(f32[8,16,32]{1,0,2:T(8,128)} %pad_maximum_fusion.8, f32[]{:T(128)} %constant.112.clone.1), padding=0_0_0x0_0_0x0_1_1 | pad | bytes 49156 | tf_op jit(solution)/shard_map/pad | solution.py:51
  347.0 1.7 add.508
  348.6 1.8 fusion.24
  350.5 2.2 slice.420
  352.7 3.1 slice.500
  357.0 1.6 fusion.21
  360.1 38.7 %pad.369 = f32[8,16,256]{1,0,2:T(8,128)} pad(f32[8,16,128]{1,0,2:T(8,128)S(1)} %add.511, f32[]{:T(128)} %constant.112.clone.1), padding=0_0_0x0_0_0x1_0_1 | pad | bytes 196612
  407.4 38.7 %pad.277 = f32[8,16,255]{1,0,2:T(8,128)} pad(f32[8,16,128]{1,0,2:T(8,128)S(1)} %pad_maximum_fusion, f32[]{:T(128)} %constant.112.clone.1), padding=0_0_0x0_0_0x0_0_1 | pad | bytes 196100 | tf_op jit(solution)/shard_map/slice | solution.py:64
  446.1 4.5 fusion
  456.0 5.7 all-to-all-start.4
  464.2 9.9 %all-to-all-done.4 = f32[128,1,128]{2,1,0:T(1,128)S(1)} async-done(((f32[128,1,128]{2,1,0:T(1,128)}), f32[128,1,128]{2,1,0:T(1,128)S(1)}, u32[]{:S(2)}, u32[]{:S(2)}) %all-to-all-start.4) | async-done | bytes 65568 | tf_op jit(solution)/shard_map/all_to_all | solution.py:151
  474.1 5.8 all-to-all-start.1
  482.3 184.7 %all_gather.3 = f32[16,1024]{0,1:T(8,128)S(1)} all-gather(f32[16,8]{0,1:T(8,128)S(1)} %multiply_multiply_fusion), channel_id=1, replica_groups=mesh['ctx'=128,'tp'=2] {'ctx'}, dimensions={1}, use_global_device_ids=true | all-gather | bytes 66048 | tf_op jit(solution)/shard_map/all_gather | solution.py:153
  (265 shorter events, 64.0 us)
Async XLA Ops:
  0.6 1.3 copy-start.20
  3.1 39.0 %all-to-all-start.2 = ((bf16[128,8,256]{2,1,0:T(8,128)(2,1)}), bf16[128,8,256]{2,1,0:T(8,128)(2,1)S(1)}, u32[]{:S(2)}, u32[]{:S(2)}) async-start(bf16[128,8,256]{2,1,0:T(8,128)(2,1)} %fusion.14), calls=%async_computation.2 | async-start | bytes 1048576 | tf_op jit(solution)/shard_map/all_to_all | solution.py:122
  21.1 129.0 %copy-start.38 = (f32[16,8]{0,1:T(8,128)}, f32[16,8]{0,1:T(8,128)S(1)}, u32[]{:S(2)}) copy-start(f32[16,8]{0,1:T(8,128)S(1)} %copy.254) | copy-start | bytes 1540
  21.1 6.9 %copy-start.40 = (s32[128,128]{1,0:T(8,128)}, s32[128,128]{1,0:T(8,128)S(1)}, u32[]{:S(2)}) copy-start(s32[128,128]{1,0:T(8,128)S(1)} %iota_subtract_fusion) | copy-start | bytes 196612
  21.1 128.5 %copy-start.36 = (f32[8,16]{1,0:T(8,128)}, f32[8,16]{1,0:T(8,128)S(1)}, u32[]{:S(2)}) copy-start(f32[8,16]{1,0:T(8,128)S(1)} %get-tuple-element.84) | copy-start | bytes 1540
  21.4 26.6 %copy-start.42 = (f32[8,16]{1,0:T(8,128)}, f32[8,16]{1,0:T(8,128)S(1)}, u32[]{:S(2)}) copy-start(f32[8,16]{1,0:T(8,128)S(1)} %get-tuple-element.86) | copy-start | bytes 1540
  21.4 26.7 %copy-start.34 = (f32[8,16]{1,0:T(8,128)}, f32[8,16]{1,0:T(8,128)S(1)}, u32[]{:S(2)}) copy-start(f32[8,16]{1,0:T(8,128)S(1)} %get-tuple-element.87) | copy-start | bytes 1540
  21.4 26.9 %copy-start.32 = (f32[8,16]{1,0:T(8,128)}, f32[8,16]{1,0:T(8,128)S(1)}, u32[]{:S(2)}) copy-start(f32[8,16]{1,0:T(8,128)S(1)} %get-tuple-element.88) | copy-start | bytes 1540
  21.4 27.1 %copy-start.30 = (f32[8,16]{1,0:T(8,128)}, f32[8,16]{1,0:T(8,128)S(1)}, u32[]{:S(2)}) copy-start(f32[8,16]{1,0:T(8,128)S(1)} %get-tuple-element.89) | copy-start | bytes 1540
  21.5 27.4 %copy-start.27 = (f32[8,16]{1,0:T(8,128)}, f32[8,16]{1,0:T(8,128)S(1)}, u32[]{:S(2)}) copy-start(f32[8,16]{1,0:T(8,128)S(1)} %get-tuple-element.90) | copy-start | bytes 1540
  47.9 1.5 copy-start.5
  49.5 2.3 slice-start
  147.7 1.4 copy-start.8
  149.0 0.7 copy-start.49
  151.4 6.9 %copy-start.21 = (bf16[256,1024]{1,0:T(8,128)(2,1)S(1)}, bf16[256,1024]{1,0:T(8,128)(2,1)}, u32[]{:S(2)}) copy-start(bf16[256,1024]{1,0:T(8,128)(2,1)} %param.7) | copy-start | bytes 1572868
  152.5 6.0 copy-start.22
  152.5 27.9 %all-to-all-start.3 = ((bf16[8,128,256]{2,0,1:T(8,128)(2,1)}), bf16[8,128,256]{2,0,1:T(8,128)(2,1)S(1)}, u32[]{:S(2)}, u32[]{:S(2)}) async-start(bf16[8,128,256]{2,0,1:T(8,128)(2,1)} %copy.217), calls=%async_computation.3 | async-start | bytes 1048576 | tf_op jit(solution)/shard_map/all_to_all | solution.py:145
  182.1 27.6 %all-to-all-start = ((bf16[128,8,256]{2,1,0:T(8,128)(2,1)}), bf16[128,8,256]{2,1,0:T(8,128)(2,1)S(1)}, u32[]{:S(2)}, u32[]{:S(2)}) async-start(bf16[128,8,256]{2,1,0:T(8,128)(2,1)} %get-tuple-element.53), calls=%async_computation | async-start | bytes 1048576 | tf_op jit(solution)/shard_map/all_to_all | solution.py:121
  187.6 2.5 copy-start.46
  210.6 145.2 %copy-start.12 = (f32[8,16,256]{2,1,0:T(8,128)}, f32[8,16,256]{2,1,0:T(8,128)S(1)}, u32[]{:S(2)}) copy-start(f32[8,16,256]{2,1,0:T(8,128)S(1)} %fusion.39) | copy-start | bytes 393220
  215.6 6.7 copy-start.13
  224.8 0.7 copy-start.28
  224.8 0.7 copy-start.31
  224.8 1.4 copy-start.33
  224.9 1.3 copy-start.35
  224.9 1.4 copy-start.43
  225.5 0.6 copy-start.23
  225.5 0.6 copy-start.24
  226.2 2.5 copy-start.25
  226.2 3.1 copy-start.26
  286.9 28.6 %copy-start.29 = (f32[8,16]{1,0:T(8,128)S(1)}, f32[8,16]{1,0:T(8,128)}, u32[]{:S(2)}) copy-start(f32[8,16]{1,0:T(8,128)} %copy-done.27) | copy-start | bytes 1540
  314.9 2.3 copy-start.14
  314.9 2.3 copy-start.15
  314.9 4.2 copy-start.45
  317.2 2.1 copy-start.19
  350.5 6.5 copy-start.9
  357.0 1.6 copy-start.18
  357.0 1.6 copy-start.44
  358.6 0.9 copy-start.16
  360.1 38.7 %copy-start.17 = (f32[8,16,63]{1,0,2:T(8,128)S(1)}, f32[8,16,63]{1,0,2:T(8,128)}, u32[]{:S(2)}) copy-start(f32[8,16,63]{1,0,2:T(8,128)} %get-tuple-element.46) | copy-start | bytes 96772
  399.3 2.6 slice-start.2
  402.0 1.1 copy-start.10
  402.0 1.2 copy-start.11
  405.2 1.0 slice-start.1
  406.2 39.8 %copy-start.41 = (s32[128,128]{1,0:T(8,128)S(1)}, s32[128,128]{1,0:T(8,128)}, u32[]{:S(2)}) copy-start(s32[128,128]{1,0:T(8,128)} %copy-done.40) | copy-start | bytes 196612
  446.1 4.9 copy-start.3
  450.9 1.2 copy-start.4
  452.2 0.7 copy-start.37
  452.2 0.7 copy-start.48
  452.9 1.2 copy-start
  452.9 1.5 copy-start.1
  455.1 6.6 copy-start.2
  455.1 6.6 copy-start.39
  455.1 6.6 copy-start.47
  456.0 18.1 %all-to-all-start.4 = ((f32[128,1,128]{2,1,0:T(1,128)}), f32[128,1,128]{2,1,0:T(1,128)S(1)}, u32[]{:S(2)}, u32[]{:S(2)}) async-start(f32[128,1,128]{2,1,0:T(1,128)} %reshape.115), calls=%async_computation.4 | async-start | bytes 131072 | tf_op jit(solution)/shard_map/all_to_all | solution.py:151
  463.1 16.8 %copy-start.7 = (bf16[256,1024]{0,1:T(8,128)(2,1)S(1)}, bf16[256,1024]{0,1:T(8,128)(2,1)}, u32[]{:S(2)}) copy-start(bf16[256,1024]{0,1:T(8,128)(2,1)} %get-tuple-element.52) | copy-start | bytes 1572868
  464.2 16.7 %copy-start.6 = (bf16[256,1024]{0,1:T(8,128)(2,1)S(1)}, bf16[256,1024]{0,1:T(8,128)(2,1)}, u32[]{:S(2)}) copy-start(bf16[256,1024]{0,1:T(8,128)(2,1)} %get-tuple-element.51) | copy-start | bytes 1572868
  474.1 196.1 %all-to-all-start.1 = ((bf16[8,128,256]{2,0,1:T(8,128)(2,1)}), bf16[8,128,256]{2,0,1:T(8,128)(2,1)S(1)}, u32[]{:S(2)}, u32[]{:S(2)}) async-start(bf16[8,128,256]{2,0,1:T(8,128)(2,1)} %copy.208), calls=%async_computation.1 | async-start | bytes 1048576 | tf_op jit(solution)/shard_map/all_to_all | solution.py:144
